TPU v7x, 32 devices: a whole 2x2x4 slice. The times are simulated.
32 devices in a mesh: pipe: 4 (over y, core), expert: 4 (over z), tensor: 2 (over x).
Axes of the slice: x: 2, y: 2, z: 4, core: 2. Of those that a mesh axis runs over, the one named last changes fastest.
Arguments:
- tokens: bfloat16 [64, 6144], P('expert', ('pipe', 'tensor')), may hold values from -6 to 6
- expert_ids: int32 [64, 2], P('expert'), may hold values from 0 to 3, all different within a row; in each aligned block of 16 rows (0 to 15, 16 to 31, ...) at most 10 rows name the same one
- gates: float32 [64, 2], P('expert'), may hold values from 0.2 to 1
- w_gate: bfloat16 [4, 6144, 8192], P('expert', None, ('pipe', 'tensor')), may hold values from -0.078125 to 0.078125
- w_up: bfloat16 [4, 6144, 8192], P('expert', None, ('pipe', 'tensor')), may hold values from -0.078125 to 0.078125
- w_down: bfloat16 [4, 8192, 6144], P('expert', ('pipe', 'tensor')), may hold values from -0.0625 to 0.0625
- d_out: bfloat16 [64, 6144], P('expert', ('pipe', 'tensor')), may hold values from -6 to 6
Outputs:
- moe_out: bfloat16 [64, 6144], P('expert', ('pipe', 'tensor'))
- grad_tokens: bfloat16 [64, 6144], P('expert', ('pipe', 'tensor'))
- grad_gates: float32 [64, 2], P('expert')
Inputs may be any that keep to these rules, and one draw needn't show every extreme that they name: `expert_ids`: each row names 2 different experts. Among the rows of one index of expert (aligned blocks of 16 rows) no expert is named more than 10 times, a bound that some block reaches.
All inputs are finite; a program needn't handle non-finite values.
Results may differ from a plain program's by a relative error of at most 0.017.
Values may be sent and summed in bfloat16 or wider, within the bound.
A program may use at most 128 MiB of HBM per device.

v0:
```python
import jax
import jax.numpy as jnp
from jax import lax
from jax.sharding import PartitionSpec as P


def per_device(tokens, expert_ids, gates, w_gate, w_up, w_down, d_out):
    tok_rows = tokens.shape[0]
    top = expert_ids.shape[1]
    devices_all = lax.axis_size("expert")
    experts = min(8, devices_all)
    group = devices_all // experts
    capacity = min(
        tok_rows,
        max(2, max(5 * tok_rows * top // (4 * experts), (tok_rows * top + experts - 1) // experts)),
    )
    slots = experts * capacity
    flat_ids = expert_ids.reshape(-1)
    onehot = (flat_ids[:, None] == jnp.arange(experts, dtype=jnp.int32)[None, :]).astype(jnp.int32)
    position = jnp.sum(jnp.cumsum(onehot, axis=0) * onehot, axis=1) - 1
    slot_of = flat_ids * capacity + position
    picks = (jnp.arange(slots, dtype=jnp.int32)[:, None] == slot_of[None, :]).astype(jnp.float32)
    pick_rows = picks.reshape(slots, tok_rows, top)
    select_tok = jnp.sum(pick_rows, axis=2).astype(jnp.bfloat16)
    select_gate = jnp.sum(pick_rows * gates[None, :, :], axis=2)
    whole_x, whole_dy = (
        lax.all_gather(tokens, ("pipe", "tensor"), axis=1, tiled=True),
        lax.all_gather(d_out, ("pipe", "tensor"), axis=1, tiled=True),
    )
    picked = jnp.dot(select_tok, whole_x, preferred_element_type=jnp.float32).astype(jnp.bfloat16)
    send_x = jnp.repeat(picked.reshape(experts, capacity, -1), group, axis=0)
    scaled = jnp.dot(select_gate, whole_dy.astype(jnp.float32), precision=lax.Precision.HIGHEST)
    send_dy = jnp.repeat(scaled.astype(jnp.bfloat16).reshape(experts, capacity, -1), group, axis=0)
    recv_x, recv_dy = (
        lax.all_to_all(send_x, "expert", split_axis=0, concat_axis=0, tiled=True),
        lax.all_to_all(send_dy, "expert", split_axis=0, concat_axis=0, tiled=True),
    )
    rows_x = recv_x.reshape(devices_all * capacity, -1)
    rows_dy = recv_dy.reshape(devices_all * capacity, -1)
    gate_proj = w_gate[0]
    up_proj = w_up[0]
    down_proj = w_down[0]
    contract_last = (((1,), (1,)), ((), ()))
    h_gate = jnp.dot(rows_x, gate_proj, preferred_element_type=jnp.float32)
    h_up = jnp.dot(rows_x, up_proj, preferred_element_type=jnp.float32)
    sig = jax.nn.sigmoid(h_gate)
    hidden = (h_gate * sig * h_up).astype(jnp.bfloat16)
    out_terms = jnp.dot(hidden, down_proj, preferred_element_type=jnp.float32)
    d_hidden = lax.dot_general(
        rows_dy, down_proj, contract_last, preferred_element_type=jnp.float32
    )
    d_gate_h = (d_hidden * h_up * sig * (1.0 + h_gate * (1.0 - sig))).astype(jnp.bfloat16)
    d_up_h = (d_hidden * h_gate * sig).astype(jnp.bfloat16)
    dx_terms = lax.dot_general(
        d_gate_h, gate_proj, contract_last, preferred_element_type=jnp.float32
    )
    dx_terms = dx_terms + lax.dot_general(
        d_up_h, up_proj, contract_last, preferred_element_type=jnp.float32
    )
    out_share, dx_share = (
        lax.psum_scatter(
            out_terms.astype(jnp.bfloat16), ("pipe", "tensor"), scatter_dimension=1, tiled=True
        ).astype(jnp.float32),
        lax.psum_scatter(
            dx_terms.astype(jnp.bfloat16), ("pipe", "tensor"), scatter_dimension=1, tiled=True
        ).astype(jnp.float32),
    )
    out_slot = out_share.reshape(devices_all, capacity, -1)
    dx_slot = dx_share.reshape(devices_all, capacity, -1)
    back_out, back_dx = (
        lax.all_to_all(
            out_slot.astype(jnp.bfloat16), "expert", split_axis=0, concat_axis=0, tiled=True
        ).astype(out_slot.dtype),
        lax.all_to_all(
            dx_slot.astype(jnp.bfloat16), "expert", split_axis=0, concat_axis=0, tiled=True
        ).astype(dx_slot.dtype),
    )
    out_rows = (
        jnp.sum(back_out.reshape(experts, group, capacity, -1), axis=1)
        .astype(jnp.bfloat16)
        .reshape(slots, -1)
    )
    dx_rows = (
        jnp.sum(back_dx.reshape(experts, group, capacity, -1), axis=1)
        .astype(jnp.bfloat16)
        .reshape(slots, -1)
    )
    assign = picks.T.astype(jnp.bfloat16)
    a_out = jnp.dot(assign, out_rows, preferred_element_type=jnp.float32)
    a_dx = jnp.dot(assign, dx_rows, preferred_element_type=jnp.float32)
    a_out = a_out.reshape(tok_rows, top, -1)
    a_dx = a_dx.reshape(tok_rows, top, -1)
    moe_out = jnp.sum(gates[:, :, None] * a_out, axis=1).astype(jnp.bfloat16)
    grad_tokens = jnp.sum(a_dx, axis=1).astype(jnp.bfloat16)
    partial_dots = jnp.sum(d_out.astype(jnp.float32)[:, None, :] * a_out, axis=2)
    grad_gates = lax.psum(partial_dots, ("pipe", "tensor"))
    return (moe_out, grad_tokens, grad_gates)


def solution(mesh):
    return jax.shard_map(
        per_device,
        mesh=mesh,
        in_specs=(
            P("expert", ("pipe", "tensor")),
            P("expert", None),
            P("expert", None),
            P("expert", None, ("pipe", "tensor")),
            P("expert", None, ("pipe", "tensor")),
            P("expert", ("pipe", "tensor"), None),
            P("expert", ("pipe", "tensor")),
        ),
        out_specs=(
            P("expert", ("pipe", "tensor")),
            P("expert", ("pipe", "tensor")),
            P("expert", None),
        ),
        check_vma=False,
    )
```

profile of v0, /device:TPU:0, one launch (start us, length us, event | category | flops | bytes accessed | tf_op | source)
XLA Modules:
  0.0 203.2 jit_solution(13085870068729165477)
XLA Ops:
  7.2 17.2 %all_gather.6 = bf16[16,6144]{1,0:T(8,128)(2,1)S(1)} all-gather(bf16[16,768]{1,0:T(8,128)(2,1)} %param.7), channel_id=1, replica_groups=mesh['pipe'=4,'expert'=4,'tensor'=2] {'pipe','tensor'}, dimensions={1}, use_global_device_ids=true | all-gather | bytes 221184 | tf_op jit(solution)/shard_map/all_gather | solution.py:27
  27.5 1.1 reshape_broadcast_in_dim_reshape.6
  28.6 4.9 %all-to-all-start = ((bf16[4,10,6144]{2,1,0:T(8,128)(2,1)}), bf16[4,10,6144]{2,1,0:T(8,128)(2,1)S(1)}, u32[]{:S(2)}, u32[]{:S(2)}) async-start(bf16[4,10,6144]{2,1,0:T(8,128)(2,1)} %reshape_broadcast_in_dim_reshape.6), calls=%async_computation | async-start | bytes 1572864 | tf_op jit(solution)/shard_map/all_to_all | solution.py:35
  33.4 16.2 %all_gather.7 = bf16[16,6144]{1,0:T(8,128)(2,1)S(1)} all-gather(bf16[16,768]{1,0:T(8,128)(2,1)} %param.13), channel_id=1, replica_groups=mesh['pipe'=4,'expert'=4,'tensor'=2] {'pipe','tensor'}, dimensions={1}, use_global_device_ids=true | all-gather | bytes 221184 | tf_op jit(solution)/shard_map/all_gather | solution.py:28
  50.2 1.1 reshape_broadcast_in_dim_reshape.7
  51.3 3.6 %all-to-all-done = bf16[4,10,6144]{2,1,0:T(8,128)(2,1)S(1)} async-done(((bf16[4,10,6144]{2,1,0:T(8,128)(2,1)}), bf16[4,10,6144]{2,1,0:T(8,128)(2,1)S(1)}, u32[]{:S(2)}, u32[]{:S(2)}) %all-to-all-start) | async-done | bytes 491552 | tf_op jit(solution)/shard_map/all_to_all | solution.py:35
  54.9 3.5 %all-to-all-start.2 = ((bf16[4,10,6144]{2,1,0:T(8,128)(2,1)}), bf16[4,10,6144]{2,1,0:T(8,128)(2,1)S(1)}, u32[]{:S(2)}, u32[]{:S(2)}) async-start(bf16[4,10,6144]{2,1,0:T(8,128)(2,1)} %reshape_broadcast_in_dim_reshape.7), calls=%async_computation.3 | async-start | bytes 1572864 | tf_op jit(solution)/shard_map/all_to_all | solution.py:36
  58.9 6.8 %fusion.6 = f32[40,1024]{1,0:T(8,128)S(1)} fusion(bf16[40,6144]{1,0:T(8,128)(2,1)S(1)} %reshape.100, bf16[1,6144,1024]{2,1,0:T(8,128)(2,1)} %param.11), kind=kOutput, calls=%fused_computation.6 | convolution fusion | flops 503316480 | bytes 13238272 | tf_op jit(solution)/shard_map/dot_general | solution.py:45
  65.7 6.8 %fusion.10 = f32[40,1024]{1,0:T(8,128)S(1)} fusion(bf16[40,6144]{1,0:T(8,128)(2,1)S(1)} %reshape.100, bf16[1,6144,1024]{2,1,0:T(8,128)(2,1)} %param.10), kind=kOutput, calls=%fused_computation.10 | convolution fusion | flops 503316480 | bytes 13238272 | tf_op jit(solution)/shard_map/dot_general | solution.py:44
  72.5 6.5 %all-to-all-done.2 = bf16[4,10,6144]{2,1,0:T(8,128)(2,1)S(1)} async-done(((bf16[4,10,6144]{2,1,0:T(8,128)(2,1)}), bf16[4,10,6144]{2,1,0:T(8,128)(2,1)S(1)}, u32[]{:S(2)}, u32[]{:S(2)}) %all-to-all-start.2) | async-done | bytes 491552 | tf_op jit(solution)/shard_map/all_to_all | solution.py:36
  79.3 8.6 %fusion = f32[40,1024]{1,0:T(8,128)S(1)} fusion(bf16[40,6144]{1,0:T(8,128)(2,1)S(1)} %reshape.101, bf16[1,1024,6144]{2,1,0:T(8,128)(2,1)} %param.12), kind=kOutput, calls=%fused_computation | convolution fusion | flops 503316480 | bytes 13238272 | tf_op jit(solution)/shard_map/dot_general | solution.py:49
  87.8 8.6 %fusion.4 = f32[40,6144]{1,0:T(8,128)S(1)} fusion(bf16[1,6144,1024]{2,1,0:T(8,128)(2,1)} %param.11, f32[40,1024]{1,0:T(8,128)S(1)} %fusion, f32[40,1024]{1,0:T(8,128)S(1)} %fusion.10), kind=kOutput, calls=%fused_computation.4 | convolution fusion | flops 503562240 | bytes 13893632 | tf_op jit(solution)/shard_map/dot_general | solution.py:57
  96.5 4.9 %fusion.15 = bf16[40,6144]{1,0:T(8,128)(2,1)} fusion(f32[40,6144]{1,0:T(8,128)S(1)} %fusion.4, bf16[1,6144,1024]{2,1,0:T(8,128)(2,1)S(1)} %bitcast.37, f32[40,1024]{1,0:T(8,128)S(1)} %fusion.10, f32[40,1024]{1,0:T(8,128)S(1)} %fusion, f32[40,1024]{1,0:T(8,128)S(1)} %fusion.6), kind=kOutput, calls=%fused_computation.13 | convolution fusion | flops 504217600 | bytes 14548992 | tf_op jit(solution)/shard_map/dot_general | solution.py:54
  101.5 7.7 %fusion.18 = bf16[40,6144]{1,0:T(8,128)(2,1)} fusion(bf16[1,1024,6144]{2,1,0:T(8,128)(2,1)} %param.12, f32[40,1024]{1,0:T(8,128)S(1)} %fusion.6, f32[40,1024]{1,0:T(8,128)S(1)} %fusion.10), kind=kOutput, calls=%fused_computation.14 | convolution fusion | flops 503808000 | bytes 13402112 | tf_op jit(solution)/shard_map/dot_general | solution.py:48
  109.2 23.8 %reduce-scatter.5.cloned.1.call-done = bf16[40,768]{1,0:T(8,128)(2,1)} async-done(((bf16[40,6144]{1,0:T(8,128)(2,1)}), bf16[40,768]{1,0:T(8,128)(2,1)}) %reduce-scatter.5.cloned.1.call-update) | async-done | bytes 61456 | tf_op jit(solution)/shard_map/reduce_scatter | solution.py:64
  133.0 1.5 convert_element_type.127
  134.5 4.6 %all-to-all-start.3 = ((bf16[4,10,768]{2,1,0:T(8,128)(2,1)}), bf16[4,10,768]{2,1,0:T(8,128)(2,1)S(1)}, u32[]{:S(2)}, u32[]{:S(2)}) async-start(bf16[4,10,768]{2,1,0:T(8,128)(2,1)} %convert_element_type.127), calls=%async_computation.5 | async-start | bytes 196608 | tf_op jit(solution)/shard_map/all_to_all | solution.py:74
  139.1 30.5 %reduce-scatter.3.cloned.1.call-done = bf16[40,768]{1,0:T(8,128)(2,1)} async-done(((bf16[40,6144]{1,0:T(8,128)(2,1)}), bf16[40,768]{1,0:T(8,128)(2,1)}) %reduce-scatter.3.cloned.1.call-update) | async-done | bytes 61456 | tf_op jit(solution)/shard_map/reduce_scatter | solution.py:61
  169.6 1.5 convert_element_type.120
  171.1 4.6 %all-to-all-start.1 = ((bf16[4,10,768]{2,1,0:T(8,128)(2,1)}), bf16[4,10,768]{2,1,0:T(8,128)(2,1)S(1)}, u32[]{:S(2)}, u32[]{:S(2)}) async-start(bf16[4,10,768]{2,1,0:T(8,128)(2,1)} %convert_element_type.120), calls=%async_computation.2 | async-start | bytes 196608 | tf_op jit(solution)/shard_map/all_to_all | solution.py:71
  175.7 0.8 convolution_reduce_fusion
  176.5 5.0 %all-to-all-done.1 = bf16[4,10,768]{2,1,0:T(8,128)(2,1)S(1)} async-done(((bf16[4,10,768]{2,1,0:T(8,128)(2,1)}), bf16[4,10,768]{2,1,0:T(8,128)(2,1)S(1)}, u32[]{:S(2)}, u32[]{:S(2)}) %all-to-all-start.1) | async-done | bytes 61472 | tf_op jit(solution)/shard_map/all_to_all | solution.py:71
  181.5 0.9 multiply_reduce_fusion
  182.4 13.9 %psum.7 = f32[16,2]{0,1:T(2,128)} all-reduce(f32[16,2]{0,1:T(2,128)S(1)} %get-tuple-element.3), channel_id=1, replica_groups=mesh['pipe'=4,'expert'=4,'tensor'=2] {'pipe','tensor'}, use_global_device_ids=true, to_apply=%region_9.10 | all-reduce | flops 32 | bytes 256 | tf_op jit(solution)/shard_map/psum | solution.py:96
  (33 shorter events, 4.4 us)
Async XLA Ops:
  28.6 26.4 %all-to-all-start = ((bf16[4,10,6144]{2,1,0:T(8,128)(2,1)}), bf16[4,10,6144]{2,1,0:T(8,128)(2,1)S(1)}, u32[]{:S(2)}, u32[]{:S(2)}) async-start(bf16[4,10,6144]{2,1,0:T(8,128)(2,1)} %reshape_broadcast_in_dim_reshape.6), calls=%async_computation | async-start | bytes 1572864 | tf_op jit(solution)/shard_map/all_to_all | solution.py:35
  54.9 24.1 %all-to-all-start.2 = ((bf16[4,10,6144]{2,1,0:T(8,128)(2,1)}), bf16[4,10,6144]{2,1,0:T(8,128)(2,1)S(1)}, u32[]{:S(2)}, u32[]{:S(2)}) async-start(bf16[4,10,6144]{2,1,0:T(8,128)(2,1)} %reshape_broadcast_in_dim_reshape.7), calls=%async_computation.3 | async-start | bytes 1572864 | tf_op jit(solution)/shard_map/all_to_all | solution.py:36
  58.4 74.6 %reduce-scatter.5.cloned.1.call-start = ((), (), s32[]{:S(2)}) async-start(), calls=%async_computation.7 | async-start | bytes 552960 | tf_op jit(solution)/shard_map/reduce_scatter | solution.py:64
  79.2 17.2 %slice-start = ((s8[12582912]{0:T(1024)(128)(4,1)}), s8[4194304]{0:T(1024)(128)(4,1)S(1)}, s32[]{:S(2)}) async-start(s8[12582912]{0:T(1024)(128)(4,1)} %bitcast.36), calls=%async_computation.8 | async-start | bytes 8388608
  79.2 17.2 %slice-start.1 = ((s8[12582912]{0:T(1024)(128)(4,1)}), s8[4194304]{0:T(1024)(128)(4,1)S(1)}, s32[]{:S(2)}) async-start(s8[12582912]{0:T(1024)(128)(4,1)} %bitcast.36), calls=%async_computation.9 | async-start | bytes 8388608
  87.8 8.6 %slice-start.2 = ((s8[12582912]{0:T(1024)(128)(4,1)}), s8[4194304]{0:T(1024)(128)(4,1)S(1)}, s32[]{:S(2)}) async-start(s8[12582912]{0:T(1024)(128)(4,1)} %bitcast.36), calls=%async_computation.10 | async-start | bytes 8388608
  101.4 37.7 %copy-start = (bf16[16,768]{1,0:T(8,128)(2,1)S(1)}, bf16[16,768]{1,0:T(8,128)(2,1)}, u32[]{:S(2)}) copy-start(bf16[16,768]{1,0:T(8,128)(2,1)} %param.13) | copy-start | bytes 73732
  101.4 80.1 %copy-start.1 = (f32[16,2]{0,1:T(2,128)S(1)}, f32[16,2]{0,1:T(2,128)}, u32[]{:S(2)}) copy-start(f32[16,2]{0,1:T(2,128)} %param.9) | copy-start | bytes 388
  101.4 68.2 %reduce-scatter.3.cloned.1.call-start = ((), (), s32[]{:S(2)}) async-start(), calls=%async_computation.6 | async-start | bytes 552960 | tf_op jit(solution)/shard_map/reduce_scatter | solution.py:61
  134.5 36.6 %all-to-all-start.3 = ((bf16[4,10,768]{2,1,0:T(8,128)(2,1)}), bf16[4,10,768]{2,1,0:T(8,128)(2,1)S(1)}, u32[]{:S(2)}, u32[]{:S(2)}) async-start(bf16[4,10,768]{2,1,0:T(8,128)(2,1)} %convert_element_type.127), calls=%async_computation.5 | async-start | bytes 196608 | tf_op jit(solution)/shard_map/all_to_all | solution.py:74
  171.1 10.4 %all-to-all-start.1 = ((bf16[4,10,768]{2,1,0:T(8,128)(2,1)}), bf16[4,10,768]{2,1,0:T(8,128)(2,1)S(1)}, u32[]{:S(2)}, u32[]{:S(2)}) async-start(bf16[4,10,768]{2,1,0:T(8,128)(2,1)} %convert_element_type.120), calls=%async_computation.2 | async-start | bytes 196608 | tf_op jit(solution)/shard_map/all_to_all | solution.py:71
Sparse Core Ops, SparseCore 0:
  101.5 31.4 reduce-scatter.4
  136.1 33.4 reduce-scatter.2
where the time goes:
time: 204 us; the launch traced here: 203 us
  waiting for transfers between devices  69.4 us (34%)
  blocking collectives  47.4 us (23%)
  matrix products  46 us (23%)
  starting transfers between devices  17.8 us (9%)
  between operations  14.2 us (7%)
  local copies, waits for them, and re-layouts  6.59 us (3%)
    reduce_scatter x1, waiting for transfers between devices, per_device(): lax.psum_scatter(out_terms.astype(jnp.bfloat16), ('pipe', 'tensor'), scat...  30.5 us
    reduce_scatter x1, waiting for transfers between devices, per_device(): lax.psum_scatter(dx_terms.astype(jnp.bfloat16), ('pipe', 'tensor'), scatt...  23.8 us
    all_gather x1, blocking collectives, per_device(): lax.all_gather(tokens, ('pipe', 'tensor'), axis=1, tiled=True)  17.2 us
    all_gather x1, blocking collectives, per_device(): lax.all_gather(d_out, ('pipe', 'tensor'), axis=1, tiled=True)  16.2 us
    psum x1, blocking collectives, per_device(): grad_gates = lax.psum(partial_dots, ('pipe', 'tensor'))  13.9 us
    dot_general x1, matrix products, per_device(): lax.dot_general(d_up_h, up_proj, contract_last, preferred_element_type=jn...  8.59 us
    dot_general x1, matrix products, per_device(): lax.dot_general(rows_dy, down_proj, contract_last, preferred_element_type...  8.56 us
    dot_general x1, matrix products, per_device(): out_terms = jnp.dot(hidden, down_proj, preferred_element_type=jnp.float32)  7.67 us
  transfers between devices with their start and end apart: 6, of which 5 were waited for; matrix products, arithmetic and copies ran while one was open for 13% of the time, Pallas kernels for 0%

commit v1 on v0

--- a/solution.py
+++ b/solution.py
@@ -1,7 +1,335 @@
+import functools
 import jax
 import jax.numpy as jnp
 from jax import lax
+from jax.experimental import pallas as pl
+from jax.experimental.pallas import tpu as pltpu
 from jax.sharding import PartitionSpec as P
+
+MESH = pl.DeviceIdType.MESH
+FLIPS = ((0, 0, 0), (1, 0, 0), (0, 1, 0), (0, 0, 1), (1, 1, 0), (1, 0, 1), (0, 1, 1), (1, 1, 1))
+OWN, C, X, Y, CX, CY, XY, CXY = range(8)
+NT = (((1,), (1,)), ((), ()))
+TN = (((0,), (0,)), ((), ()))
+F32, BF16 = jnp.float32, jnp.bfloat16
+
+
+def layer_kernel(
+    cap, pipe_n, expert_n, tensor_n,
+    tok_ref, ids_ref, gates_ref, wg_ref, wu_ref, wd_ref, dout_ref,
+    moe_ref, gtok_ref, ggate_ref,
+    wg, wu, wd, send_a, recv_a, blocks, hg, hu, dh, hid, dgh, duh,
+    to_core, from_core, keep, diag_out, diag_in, part_x, part_y, from_x, from_y,
+    q_out, q_in, qz_out, qz_in, send_e, recv_e,
+    w_sem, as_sem, ar_sem, gs_sem, gr_sem, cs_sem, cr_sem, ds_sem, dr_sem, fs_sem, fr_sem,
+    qs_sem, qr_sem, zs_sem, zr_sem, es_sem, er_sem,
+):
+    p = lax.axis_index("pipe")
+    z = lax.axis_index("expert")
+    t = lax.axis_index("tensor")
+    toks, feat = tok_ref.shape
+    rows = expert_n * cap
+    span = 2 * toks
+    hidn = wg.shape[2]
+
+    def plane(r):
+        fc, fx, fy = FLIPS[r]
+        core, y = lax.rem(p, 2), lax.div(p, 2)
+        core = 1 - core if fc else core
+        y = 1 - y if fy else y
+        return y * 2 + core, (1 - t if fx else t)
+
+    def at_plane(r):
+        pp, tt = plane(r)
+        return {"pipe": pp, "expert": z, "tensor": tt}
+
+    def at_z(step):
+        return {"pipe": p, "expert": lax.rem(z + step, expert_n), "tensor": t}
+
+    loads = []
+    for r in range(8):
+        pp, tt = plane(r)
+        off = pl.multiple_of((pp * tensor_n + tt) * feat, feat)
+        three = (
+            pltpu.make_async_copy(wg_ref.at[0, pl.ds(off, feat), :], wg.at[r], w_sem.at[r, 0]),
+            pltpu.make_async_copy(wu_ref.at[0, pl.ds(off, feat), :], wu.at[r], w_sem.at[r, 1]),
+            pltpu.make_async_copy(wd_ref.at[0, :, pl.ds(off, feat)], wd.at[r], w_sem.at[r, 2]),
+        )
+        for copy in three:
+            copy.start()
+        loads.append(three)
+
+    barrier = pltpu.get_barrier_semaphore()
+    for r in range(1, 8):
+        pl.semaphore_signal(barrier, inc=1, device_id=at_plane(r), device_id_type=MESH)
+    for step in range(1, expert_n):
+        pl.semaphore_signal(barrier, inc=1, device_id=at_z(step), device_id_type=MESH)
+
+    def remote(src, dst, ssem, rsem, where):
+        return pltpu.make_async_remote_copy(
+            src_ref=src, dst_ref=dst, send_sem=ssem, recv_sem=rsem,
+            device_id=where, device_id_type=MESH,
+        )
+
+    lanes = expert_n * span
+    lane = lax.broadcasted_iota(jnp.int32, (toks, lanes), 1)
+    id0, id1 = ids_ref[:, 0:1], ids_ref[:, 1:2]
+    g0, g1 = gates_ref[:, 0:1], gates_ref[:, 1:2]
+    names = jnp.where((lane == id0) | (lane == id1), 1.0, 0.0).astype(BF16)
+    earlier = jnp.where(
+        lax.broadcasted_iota(jnp.int32, (toks, toks), 0) > lax.broadcasted_iota(jnp.int32, (toks, toks), 1),
+        1.0, 0.0,
+    ).astype(BF16)
+    before = jnp.dot(earlier, names, preferred_element_type=F32)
+    pos0 = jnp.sum(jnp.where(lane == id0, before, 0.0), axis=1, keepdims=True).astype(jnp.int32)
+    pos1 = jnp.sum(jnp.where(lane == id1, before, 0.0), axis=1, keepdims=True).astype(jnp.int32)
+    a0 = id0 * span + pos0
+    a1 = id1 * span + pos1
+
+    def hot(mask):
+        return jnp.where(mask, 1.0, 0.0)
+
+    pick = jnp.concatenate(
+        [hot((lane == a0) | (lane == a1)), hot(lane == a0 + toks), hot(lane == a1 + toks)], axis=0
+    ).astype(BF16)
+    d_out = dout_ref[...].astype(F32)
+    source = jnp.concatenate([tok_ref[...].astype(F32), g0 * d_out, g1 * d_out], axis=0).astype(BF16)
+    send_a[...] = lax.dot_general(pick, source, TN, preferred_element_type=F32).astype(BF16)
+    hg[...] = jnp.zeros_like(hg)
+    hu[...] = jnp.zeros_like(hu)
+    dh[...] = jnp.zeros_like(dh)
+
+    pl.semaphore_wait(barrier, 7 + expert_n - 1)
+
+    mine = pl.ds(pl.multiple_of(z * span, span), span)
+    sends = []
+    dispatch = []
+    for step in (2, 1, 3) if expert_n == 4 else range(1, expert_n):
+        to = pl.ds(pl.multiple_of(lax.rem(z + step, expert_n) * span, span), span)
+        copy = remote(send_a.at[to], recv_a.at[mine], as_sem.at[step - 1], ar_sem.at[step - 1], at_z(step))
+        copy.start()
+        sends.append(copy)
+        dispatch.append(copy)
+    recv_a[mine, :] = send_a[mine, :]
+
+    tgt = lax.broadcasted_iota(jnp.int32, (2 * rows, lanes), 0)
+    src = lax.broadcasted_iota(jnp.int32, (2 * rows, lanes), 1)
+    slot = lax.rem(src, toks)
+    home = lax.div(lax.rem(src, span), toks) * rows + lax.div(src, span) * cap + slot
+    pack = hot((tgt == home) & (slot < cap)).astype(BF16)
+    for copy in dispatch:
+        copy.wait_recv()
+    blocks[OWN] = jnp.dot(pack, recv_a[...], preferred_element_type=F32).astype(BF16)
+
+    xr = (rows + 15) // 16 * 16
+    top, low = pl.ds(0, xr), pl.ds(xr, 2 * rows - xr)
+
+    def gather(src, dst, k, r):
+        copy = remote(src, dst, gs_sem.at[k], gr_sem.at[k], at_plane(r))
+        copy.start()
+        sends.append(copy)
+        return copy
+
+    step_n = min(512, hidn)
+
+    def forward(r):
+        for copy in loads[r]:
+            copy.wait()
+        xs = blocks[r, 0:xr, :]
+        ys = blocks[r, 2 * rows - xr : 2 * rows, :]
+
+        def body(n, carry):
+            cols = pl.ds(pl.multiple_of(n * step_n, step_n), step_n)
+            hg[:, cols] += jnp.dot(xs, wg[r, :, cols], preferred_element_type=F32)
+            hu[:, cols] += jnp.dot(xs, wu[r, :, cols], preferred_element_type=F32)
+            dh[:, cols] += lax.dot_general(ys, wd[r, cols, :], NT, preferred_element_type=F32)
+            return carry
+
+        lax.fori_loop(0, hidn // step_n, body, 0)
+
+    on_x = gather(blocks.at[OWN], blocks.at[X], 0, X)
+    on_y = gather(blocks.at[OWN], blocks.at[Y], 1, Y)
+    on_c = gather(blocks.at[OWN], blocks.at[C], 2, C)
+    forward(OWN)
+    on_c.wait_recv()
+    forward(C)
+    on_x.wait_recv()
+    low_xy = gather(blocks.at[X, low], blocks.at[XY, low], 3, Y)
+    on_cx = gather(blocks.at[X], blocks.at[CX], 4, C)
+    on_y.wait_recv()
+    top_xy = gather(blocks.at[Y, top], blocks.at[XY, top], 5, X)
+    on_cy = gather(blocks.at[Y], blocks.at[CY], 6, C)
+    forward(X)
+    forward(Y)
+    low_xy.wait_recv()
+    top_xy.wait_recv()
+    on_cxy = gather(blocks.at[XY], blocks.at[CXY], 7, C)
+    on_cx.wait_recv()
+    forward(CX)
+    on_cy.wait_recv()
+    forward(CY)
+    forward(XY)
+    on_cxy.wait_recv()
+    forward(CXY)
+
+    h_gate, h_up = hg[0:rows, :], hu[0:rows, :]
+    d_hidden = dh[xr - rows : xr, :]
+    sig = jax.nn.sigmoid(h_gate)
+    hidden = h_gate * sig * h_up
+    hid[...] = hidden.astype(BF16)
+    dgh[...] = (d_hidden * h_up * sig * (1.0 + h_gate * (1.0 - sig))).astype(BF16)
+    duh[...] = (d_hidden * h_gate * sig).astype(BF16)
+    inner = jnp.sum(hidden * d_hidden, axis=1, keepdims=True)
+    diagonal = lax.broadcasted_iota(jnp.int32, (rows, 128), 0) == lax.broadcasted_iota(jnp.int32, (rows, 128), 1)
+    q_row = jnp.sum(jnp.where(diagonal, inner, 0.0), axis=0, keepdims=True)
+    q_out[...] = jnp.broadcast_to(q_row, q_out.shape)
+    me = p * tensor_n + t
+    q_in[me] = q_out[...]
+    q_copies = []
+
+    def partial(r):
+        out = jnp.dot(hid[...], wd[r], preferred_element_type=F32)
+        dx = lax.dot_general(dgh[...], wg[r], NT, preferred_element_type=F32)
+        dx = dx + lax.dot_general(duh[...], wu[r], NT, preferred_element_type=F32)
+        return jnp.concatenate([out, dx], axis=0)
+
+    def core_share(i, r):
+        to_core[i] = partial(r).astype(BF16)
+        copy = remote(to_core.at[i], from_core.at[i], cs_sem.at[i], cr_sem.at[i], at_plane(C))
+        copy.start()
+        sends.append(copy)
+        return copy
+
+    def chip_sum(i, copy):
+        copy.wait_recv()
+        return keep[...] + from_core[i].astype(F32)
+
+    def ship(src, dst, ssem, rsem, r):
+        copy = remote(src, dst, ssem, rsem, at_plane(r))
+        copy.start()
+        sends.append(copy)
+        return copy
+
+    s0 = core_share(0, CXY)
+    for r in range(1, 8):
+        copy = remote(q_out, q_in.at[me], qs_sem.at[r - 1], qr_sem.at[r - 1], at_plane(r))
+        copy.start()
+        sends.append(copy)
+        q_copies.append(copy)
+    keep[...] = partial(XY)
+    s1 = core_share(1, CX)
+    diag_out[...] = chip_sum(0, s0).astype(BF16)
+    diag_x = ship(diag_out.at[top], diag_in.at[top], ds_sem.at[0], dr_sem.at[0], X)
+    diag_y = ship(diag_out.at[low], diag_in.at[low], ds_sem.at[1], dr_sem.at[1], Y)
+    keep[...] = partial(X)
+    s2 = core_share(2, CY)
+    part_x[...] = chip_sum(1, s1)
+    keep[...] = partial(Y)
+    diag_out_x = part_x[0:xr, :].astype(BF16)
+    to_core[4, 0:xr, :] = diag_out_x
+    x_top = ship(to_core.at[4, top], from_x.at[top], fs_sem.at[0], fr_sem.at[0], X)
+    s3 = core_share(3, C)
+    part_y[...] = chip_sum(2, s2)
+    to_core[5, xr : 2 * rows, :] = part_y[xr : 2 * rows, :].astype(BF16)
+    y_low = ship(to_core.at[5, low], from_y.at[low], fs_sem.at[1], fr_sem.at[1], Y)
+    diag_x.wait_recv()
+    to_core[5, 0:xr, :] = (part_y[0:xr, :] + diag_in[0:xr, :].astype(F32)).astype(BF16)
+    y_top = ship(to_core.at[5, top], from_y.at[top], fs_sem.at[2], fr_sem.at[2], Y)
+    diag_y.wait_recv()
+    to_core[4, xr : 2 * rows, :] = (
+        part_x[xr : 2 * rows, :] + diag_in[xr : 2 * rows, :].astype(F32)
+    ).astype(BF16)
+    x_low = ship(to_core.at[4, low], from_x.at[low], fs_sem.at[3], fr_sem.at[3], X)
+    keep[...] = partial(OWN)
+    keep[...] = chip_sum(3, s3)
+
+    for copy in q_copies:
+        copy.wait_recv()
+    total_q = q_in[0]
+    for j in range(1, 8):
+        total_q = total_q + q_in[j]
+    qz_out[...] = total_q
+    qz_in[z] = total_q
+    back = []
+    for step in range(1, expert_n):
+        copy = remote(qz_out, qz_in.at[z], zs_sem.at[step - 1], zr_sem.at[step - 1], at_z(step))
+        copy.start()
+        sends.append(copy)
+        back.append(copy)
+
+    for copy in (x_top, y_low, y_top, x_low):
+        copy.wait_recv()
+    final = (keep[...] + from_x[...].astype(F32) + from_y[...].astype(F32)).astype(BF16)
+    send_e[...] = lax.dot_general(pack, final, TN, preferred_element_type=F32).astype(BF16)
+    for step in (2, 1, 3) if expert_n == 4 else range(1, expert_n):
+        to = pl.ds(pl.multiple_of(lax.rem(z + step, expert_n) * span, span), span)
+        copy = remote(send_e.at[to], recv_e.at[mine], es_sem.at[step - 1], er_sem.at[step - 1], at_z(step))
+        copy.start()
+        sends.append(copy)
+        back.append(copy)
+    recv_e[mine, :] = send_e[mine, :]
+    take = jnp.concatenate(
+        [hot(lane == a0), hot(lane == a1), hot((lane == a0 + toks) | (lane == a1 + toks))], axis=0
+    ).astype(BF16)
+    for copy in back:
+        copy.wait_recv()
+    got = jnp.dot(take, recv_e[...], preferred_element_type=F32)
+    moe_ref[...] = (g0 * got[0:toks] + g1 * got[toks : 2 * toks]).astype(moe_ref.dtype)
+    gtok_ref[...] = got[2 * toks : 3 * toks].astype(gtok_ref.dtype)
+    place = lax.broadcasted_iota(jnp.int32, (toks, 128), 1) - z * cap
+    sum0 = jnp.zeros((toks, 1), F32)
+    sum1 = jnp.zeros((toks, 1), F32)
+    for e in range(expert_n):
+        row = qz_in[e][0:1, :]
+        sum0 += jnp.sum(jnp.where((id0 == e) & (place == pos0), row, 0.0), axis=1, keepdims=True)
+        sum1 += jnp.sum(jnp.where((id1 == e) & (place == pos1), row, 0.0), axis=1, keepdims=True)
+    two = lax.broadcasted_iota(jnp.int32, (toks, 2), 1)
+    ggate_ref[...] = jnp.where(two == 0, sum0 / g0, sum1 / g1)
+    for copy in sends:
+        copy.wait_send()
+
+
+def fused(cap, pipe_n, expert_n, tensor_n, tokens, expert_ids, gates, w_gate, w_up, w_down, d_out):
+    toks, feat = tokens.shape
+    hidn = w_gate.shape[2]
+    rows = expert_n * cap
+    xr = (rows + 15) // 16 * 16
+    span = 2 * toks
+    vm = lambda *shape: pltpu.VMEM(shape, BF16)
+    vf = lambda *shape: pltpu.VMEM(shape, F32)
+    dma = lambda *shape: pltpu.SemaphoreType.DMA(shape)
+    inside, outside = pl.BlockSpec(memory_space=pltpu.VMEM), pl.BlockSpec(memory_space=pl.ANY)
+    return pl.pallas_call(
+        functools.partial(layer_kernel, cap, pipe_n, expert_n, tensor_n),
+        out_shape=(
+            jax.ShapeDtypeStruct(tokens.shape, BF16),
+            jax.ShapeDtypeStruct(tokens.shape, BF16),
+            jax.ShapeDtypeStruct(gates.shape, F32),
+        ),
+        in_specs=[inside, inside, inside, outside, outside, outside, inside],
+        out_specs=(inside, inside, inside),
+        scratch_shapes=[
+            vm(8, feat, hidn), vm(8, feat, hidn), vm(8, hidn, feat),
+            vm(expert_n * span, feat), vm(expert_n * span, feat), vm(8, 2 * rows, feat),
+            vf(xr, hidn), vf(xr, hidn), vf(xr, hidn),
+            vm(rows, hidn), vm(rows, hidn), vm(rows, hidn),
+            vm(6, 2 * rows, feat), vm(4, 2 * rows, feat), vf(2 * rows, feat),
+            vm(2 * rows, feat), vm(2 * rows, feat), vf(2 * rows, feat), vf(2 * rows, feat),
+            vm(2 * rows, feat), vm(2 * rows, feat),
+            vf(8, 128), vf(8, 8, 128), vf(8, 128), vf(expert_n, 8, 128),
+            vm(expert_n * span, feat), vm(expert_n * span, feat),
+            dma(8, 3), dma(expert_n - 1), dma(expert_n - 1), dma(8), dma(8), dma(4), dma(4),
+            dma(2), dma(2), dma(4), dma(4), dma(7), dma(7), dma(expert_n - 1), dma(expert_n - 1),
+            dma(expert_n - 1), dma(expert_n - 1),
+        ],
+        compiler_params=pltpu.CompilerParams(
+            collective_id=0, has_side_effects=True, vmem_limit_bytes=56 * 1024 * 1024
+        ),
+        cost_estimate=pl.CostEstimate(
+            flops=12 * rows * 8 * feat * hidn, bytes_accessed=48 * feat * hidn, transcendentals=rows * hidn
+        ),
+        name="moe_layer",
+    )(tokens, expert_ids, gates, w_gate, w_up, w_down, d_out)
 
 
 def per_device(tokens, expert_ids, gates, w_gate, w_up, w_down, d_out):
@@ -98,8 +426,19 @@
 
 
 def solution(mesh):
+    pipe_n, expert_n, tensor_n = mesh.shape["pipe"], mesh.shape["expert"], mesh.shape["tensor"]
+
+    def layer(*args):
+        toks, top = args[1].shape
+        cap = min(toks, max(2, max(5 * toks * top // (4 * expert_n), (toks * top + expert_n - 1) // expert_n)))
+        rows = expert_n * cap
+        fits = pipe_n == 4 and tensor_n == 2 and top == 2 and expert_n == 4
+        if fits and toks % 16 == 0 and rows % 8 == 0 and rows <= 128:
+            return fused(cap, pipe_n, expert_n, tensor_n, *args)
+        return per_device(*args)
+
     return jax.shard_map(
-        per_device,
+        layer,
         mesh=mesh,
         in_specs=(
             P("expert", ("pipe", "tensor")),

time: 204 us -> 51.7 us (0.25)
  waiting for transfers between devices: 69.4 us -> 0 us
  blocking collectives: 47.4 us -> 0 us
  matrix products: 46 us -> 0 us
  Pallas kernels: 0 us -> 43.9 us
  starting transfers between devices: 17.8 us -> 0 us
  between operations: 14.2 us -> 0.64 us
    reduce_scatter x2 -> x0, waiting for transfers between devices: 54.3 us -> none  [the longest x1 30.5 us: per_device(): lax.psum_scatter(out_terms.astype(jnp.bfloat16), ('pipe', 'tensor'), scat...]
    dot_general x10 -> x0, matrix products: 46 us -> none  [the longest x1 8.59 us: per_device(): lax.dot_general(d_up_h, up_proj, contract_last, preferred_element_type=jn...]
    pallas_call x0 -> x1, Pallas kernels: none -> 43.9 us  [fused(): pl.pallas_call(functools.partial(layer_kernel, cap, pipe_n, expert_n, ten...]
    all_gather x2 -> x0, blocking collectives: 33.4 us -> none  [the longest x1 17.2 us: per_device(): lax.all_gather(tokens, ('pipe', 'tensor'), axis=1, tiled=True)]
    all_to_all x4 -> x0, starting transfers between devices: 17.6 us -> none  [the longest x1 4.87 us: per_device(): lax.all_to_all(send_x, 'expert', split_axis=0, concat_axis=0, tiled=True)]
    all_to_all x4 -> x0, waiting for transfers between devices: 15.1 us -> none  [the longest x1 6.49 us: per_device(): lax.all_to_all(send_dy, 'expert', split_axis=0, concat_axis=0, tiled=True)]
    psum x1 -> x0, blocking collectives: 13.9 us -> none  [per_device(): grad_gates = lax.psum(partial_dots, ('pipe', 'tensor'))]
    unnamed x11 -> x4, local copies, waits for them, and re-layouts: 0.79 us -> 5.4 us
  transfers between devices with their start and end apart: 6 -> 0, of which waited for: 5 -> 0; matrix products, arithmetic and copies ran while one was open for 13% -> 0% of each run, Pallas kernels for 0% -> 0%
where the time goes in v1:
time: 51.7 us; the launch traced here: 51.3 us
  Pallas kernels  43.9 us (85%)
  local copies, waits for them, and re-layouts  6.73 us (13%)
  between operations  0.64 us (1%)
    pallas_call x1, Pallas kernels, fused(): pl.pallas_call(functools.partial(layer_kernel, cap, pipe_n, expert_n, ten...  43.9 us
    unnamed x4, local copies, waits for them, and re-layouts  5.4 us
    pallas_call x1, local copies, waits for them, and re-layouts, fused(): pl.pallas_call(functools.partial(layer_kernel, cap, pipe_n, expert_n, ten...  1.33 us

profile of v1, /device:TPU:0, one launch (start us, length us, event | category | flops | bytes accessed | tf_op | source)
XLA Modules:
  0.0 51.3 jit_solution(10000966993523911688)
XLA Ops:
  0.6 1.4 %copy.10.ids_ref = s32[16,2]{1,0:T(8,128)} copy(s32[16,2]{0,1:T(2,128)} %param.8) | data formatting | bytes 256 | tf_op args[1]
  2.0 1.4 %copy.11.gates_ref = f32[16,2]{1,0:T(8,128)} copy(f32[16,2]{0,1:T(2,128)} %param.9) | data formatting | bytes 256 | tf_op args[2]
  3.3 43.9 %moe_layer.1 = (bf16[16,768]{1,0:T(8,128)(2,1)}, bf16[16,768]{1,0:T(8,128)(2,1)}, f32[16,2]{1,0:T(8,128)}) custom-call(bf16[16,768]{1,0:T(8,128)(2,1)} %tok_ref.1, s32[16,2]{1,0:T(8,128)} %copy.10.ids_ref, f32[16,2]{1,0:T(8,128)} %copy.11.gates_ref, bf16[1,6144,1024]{2,1,0:T(8,128)(2,1)} %wg_ref.1, bf16[1,6144,1024]{2,1,0:T(8,128)(2,1)} %wu_ref.1, ...), custom_call_target="tpu_custom_call" | custom-call | flops 3019898880 | bytes 37748736 | tf_op jit(solution)/shard_map/moe_layer/pallas_call | solution.py:302
  47.2 1.3 %copy.12 = f32[16,2]{0,1:T(2,128)} copy(f32[16,2]{1,0:T(8,128)} %get-tuple-element.5) | data formatting | bytes 256 | tf_op jit(solution)/shard_map/moe_layer/pallas_call | solution.py:302
  48.6 1.3 %copy.15 = bf16[16,768]{1,0:T(8,128)(2,1)} copy(bf16[16,768]{1,0:T(8,128)(2,1)} %get-tuple-element.9) | data formatting | bytes 49152
  49.9 1.3 %copy.16 = bf16[16,768]{1,0:T(8,128)(2,1)} copy(bf16[16,768]{1,0:T(8,128)(2,1)} %get-tuple-element.10) | data formatting | bytes 49152

commit v2 on v1

--- a/solution.py
+++ b/solution.py
@@ -55,9 +55,14 @@
             pltpu.make_async_copy(wu_ref.at[0, pl.ds(off, feat), :], wu.at[r], w_sem.at[r, 1]),
             pltpu.make_async_copy(wd_ref.at[0, :, pl.ds(off, feat)], wd.at[r], w_sem.at[r, 2]),
         )
-        for copy in three:
-            copy.start()
         loads.append(three)
+
+    def load(first, last):
+        for three in loads[first:last]:
+            for copy in three:
+                copy.start()
+
+    load(0, 2)
 
     barrier = pltpu.get_barrier_semaphore()
     for r in range(1, 8):
@@ -71,10 +76,19 @@
             device_id=where, device_id_type=MESH,
         )
 
+    eye = lax.broadcasted_iota(jnp.int32, (toks, toks), 0) == lax.broadcasted_iota(jnp.int32, (toks, toks), 1)
+
+    def column(row):
+        return jnp.sum(jnp.where(eye, row, 0.0), axis=1, keepdims=True)
+
+    piece = send_a.shape[1] - feat
+    cuts = feat // piece
+    rest = 2 * cap - toks
     lanes = expert_n * span
     lane = lax.broadcasted_iota(jnp.int32, (toks, lanes), 1)
-    id0, id1 = ids_ref[:, 0:1], ids_ref[:, 1:2]
-    g0, g1 = gates_ref[:, 0:1], gates_ref[:, 1:2]
+    ids = ids_ref[...].astype(F32)
+    id0, id1 = column(ids[0:1]).astype(jnp.int32), column(ids[1:2]).astype(jnp.int32)
+    g0, g1 = column(gates_ref[0:1, :]), column(gates_ref[1:2, :])
     names = jnp.where((lane == id0) | (lane == id1), 1.0, 0.0).astype(BF16)
     earlier = jnp.where(
         lax.broadcasted_iota(jnp.int32, (toks, toks), 0) > lax.broadcasted_iota(jnp.int32, (toks, toks), 1),
@@ -90,36 +104,58 @@
         return jnp.where(mask, 1.0, 0.0)
 
     pick = jnp.concatenate(
-        [hot((lane == a0) | (lane == a1)), hot(lane == a0 + toks), hot(lane == a1 + toks)], axis=0
+        [hot((lane == a0) | (lane == a1)), hot(lane == a0 + cap), hot(lane == a1 + cap)], axis=0
     ).astype(BF16)
     d_out = dout_ref[...].astype(F32)
     source = jnp.concatenate([tok_ref[...].astype(F32), g0 * d_out, g1 * d_out], axis=0).astype(BF16)
-    send_a[...] = lax.dot_general(pick, source, TN, preferred_element_type=F32).astype(BF16)
+    slots = lax.dot_general(pick, source, TN, preferred_element_type=F32).astype(BF16)
+    for e in range(expert_n):
+        send_a[e * toks : (e + 1) * toks, 0:feat] = slots[e * span : e * span + toks]
+    msg = lax.broadcasted_iota(jnp.int32, (expert_n * toks, lanes), 0)
+    slot_lane = lax.broadcasted_iota(jnp.int32, (expert_n * toks, lanes), 1)
+    beside = jnp.zeros((expert_n * toks, piece), F32)
+    for c in range(cuts):
+        j = lax.rem(msg, toks) - c * rest
+        fold = hot((j >= 0) & (j < rest) & (slot_lane == lax.div(msg, toks) * span + toks + j)).astype(BF16)
+        beside = beside + jnp.dot(fold, slots[:, c * piece : (c + 1) * piece], preferred_element_type=F32)
+    send_a[:, feat:] = beside.astype(BF16)
     hg[...] = jnp.zeros_like(hg)
     hu[...] = jnp.zeros_like(hu)
     dh[...] = jnp.zeros_like(dh)
 
     pl.semaphore_wait(barrier, 7 + expert_n - 1)
 
-    mine = pl.ds(pl.multiple_of(z * span, span), span)
+    mine = pl.ds(pl.multiple_of(z * toks, toks), toks)
     sends = []
     dispatch = []
     for step in (2, 1, 3) if expert_n == 4 else range(1, expert_n):
-        to = pl.ds(pl.multiple_of(lax.rem(z + step, expert_n) * span, span), span)
+        to = pl.ds(pl.multiple_of(lax.rem(z + step, expert_n) * toks, toks), toks)
         copy = remote(send_a.at[to], recv_a.at[mine], as_sem.at[step - 1], ar_sem.at[step - 1], at_z(step))
         copy.start()
         sends.append(copy)
         dispatch.append(copy)
+    load(2, 5)
     recv_a[mine, :] = send_a[mine, :]
 
-    tgt = lax.broadcasted_iota(jnp.int32, (2 * rows, lanes), 0)
-    src = lax.broadcasted_iota(jnp.int32, (2 * rows, lanes), 1)
-    slot = lax.rem(src, toks)
-    home = lax.div(lax.rem(src, span), toks) * rows + lax.div(src, span) * cap + slot
-    pack = hot((tgt == home) & (slot < cap)).astype(BF16)
+    tgt = lax.broadcasted_iota(jnp.int32, (2 * rows, expert_n * toks), 0)
+    src = lax.broadcasted_iota(jnp.int32, (2 * rows, expert_n * toks), 1)
+    e_src, n_src = lax.div(src, toks), lax.rem(src, toks)
+    pack = hot(tgt == e_src * cap + n_src + jnp.where(n_src < cap, 0, rows - cap)).astype(BF16)
+    unfold = []
+    for c in range(cuts):
+        j = n_src - c * rest
+        unfold.append(
+            hot((j >= 0) & (j < rest) & (tgt == rows - cap + e_src * cap + toks + j)).astype(BF16)
+        )
+
+    def unpack(main, folded, message):
+        out = jnp.dot(main, message[:, 0:feat], preferred_element_type=F32)
+        extra = [jnp.dot(m, message[:, feat:], preferred_element_type=F32) for m in folded]
+        return out + (jnp.concatenate(extra, axis=1) if cuts > 1 else extra[0])
+
     for copy in dispatch:
         copy.wait_recv()
-    blocks[OWN] = jnp.dot(pack, recv_a[...], preferred_element_type=F32).astype(BF16)
+    blocks[OWN] = unpack(pack, unfold, recv_a[...]).astype(BF16)
 
     xr = (rows + 15) // 16 * 16
     top, low = pl.ds(0, xr), pl.ds(xr, 2 * rows - xr)
@@ -147,17 +183,22 @@
 
         lax.fori_loop(0, hidn // step_n, body, 0)
 
-    on_x = gather(blocks.at[OWN], blocks.at[X], 0, X)
-    on_y = gather(blocks.at[OWN], blocks.at[Y], 1, Y)
+    x_first = gather(blocks.at[OWN, low], blocks.at[X, low], 0, X)
+    y_first = gather(blocks.at[OWN, top], blocks.at[Y, top], 1, Y)
+    x_then = gather(blocks.at[OWN, top], blocks.at[X, top], 8, X)
+    y_then = gather(blocks.at[OWN, low], blocks.at[Y, low], 9, Y)
     on_c = gather(blocks.at[OWN], blocks.at[C], 2, C)
+    load(5, 8)
     forward(OWN)
+    x_first.wait_recv()
+    low_xy = gather(blocks.at[X, low], blocks.at[XY, low], 3, Y)
+    y_first.wait_recv()
+    top_xy = gather(blocks.at[Y, top], blocks.at[XY, top], 5, X)
     on_c.wait_recv()
     forward(C)
-    on_x.wait_recv()
-    low_xy = gather(blocks.at[X, low], blocks.at[XY, low], 3, Y)
+    x_then.wait_recv()
     on_cx = gather(blocks.at[X], blocks.at[CX], 4, C)
-    on_y.wait_recv()
-    top_xy = gather(blocks.at[Y, top], blocks.at[XY, top], 5, X)
+    y_then.wait_recv()
     on_cy = gather(blocks.at[Y], blocks.at[CY], 6, C)
     forward(X)
     forward(Y)
@@ -260,20 +301,35 @@
     for copy in (x_top, y_low, y_top, x_low):
         copy.wait_recv()
     final = (keep[...] + from_x[...].astype(F32) + from_y[...].astype(F32)).astype(BF16)
-    send_e[...] = lax.dot_general(pack, final, TN, preferred_element_type=F32).astype(BF16)
+    send_e[:, 0:feat] = lax.dot_general(pack, final, TN, preferred_element_type=F32).astype(BF16)
+    beside = jnp.zeros((expert_n * toks, piece), F32)
+    for c in range(cuts):
+        part = final[:, c * piece : (c + 1) * piece]
+        beside = beside + lax.dot_general(unfold[c], part, TN, preferred_element_type=F32)
+    send_e[:, feat:] = beside.astype(BF16)
     for step in (2, 1, 3) if expert_n == 4 else range(1, expert_n):
-        to = pl.ds(pl.multiple_of(lax.rem(z + step, expert_n) * span, span), span)
+        to = pl.ds(pl.multiple_of(lax.rem(z + step, expert_n) * toks, toks), toks)
         copy = remote(send_e.at[to], recv_e.at[mine], es_sem.at[step - 1], er_sem.at[step - 1], at_z(step))
         copy.start()
         sends.append(copy)
         back.append(copy)
     recv_e[mine, :] = send_e[mine, :]
-    take = jnp.concatenate(
-        [hot(lane == a0), hot(lane == a1), hot((lane == a0 + toks) | (lane == a1 + toks))], axis=0
-    ).astype(BF16)
+    at = lax.broadcasted_iota(jnp.int32, (toks, expert_n * toks), 1)
+
+    def taken(c):
+        def one(e, n):
+            if c is None:
+                return (n < toks) & (at == e * toks + n)
+            return (n >= toks) & (at == e * toks + n - toks + c * rest)
+
+        return jnp.concatenate(
+            [hot(one(id0, pos0)), hot(one(id1, pos1)), hot(one(id0, pos0 + cap) | one(id1, pos1 + cap))], axis=0
+        ).astype(BF16)
+
+    take, take_folded = taken(None), [taken(c) for c in range(cuts)]
     for copy in back:
         copy.wait_recv()
-    got = jnp.dot(take, recv_e[...], preferred_element_type=F32)
+    got = unpack(take, take_folded, recv_e[...])
     moe_ref[...] = (g0 * got[0:toks] + g1 * got[toks : 2 * toks]).astype(moe_ref.dtype)
     gtok_ref[...] = got[2 * toks : 3 * toks].astype(gtok_ref.dtype)
     place = lax.broadcasted_iota(jnp.int32, (toks, 128), 1) - z * cap
@@ -283,10 +339,26 @@
         row = qz_in[e][0:1, :]
         sum0 += jnp.sum(jnp.where((id0 == e) & (place == pos0), row, 0.0), axis=1, keepdims=True)
         sum1 += jnp.sum(jnp.where((id1 == e) & (place == pos1), row, 0.0), axis=1, keepdims=True)
-    two = lax.broadcasted_iota(jnp.int32, (toks, 2), 1)
-    ggate_ref[...] = jnp.where(two == 0, sum0 / g0, sum1 / g1)
+    ggate_ref[0:1, :] = jnp.sum(jnp.where(eye, sum0 / g0, 0.0), axis=0, keepdims=True)
+    ggate_ref[1:2, :] = jnp.sum(jnp.where(eye, sum1 / g1, 0.0), axis=0, keepdims=True)
     for copy in sends:
         copy.wait_send()
+
+
+def finish_kernel(a, b, c, out_a, out_b, out_c, sem):
+    copies = [
+        pltpu.make_async_copy(src, dst, sem.at[i])
+        for i, (src, dst) in enumerate(((a, out_a), (b, out_b), (c, out_c)))
+    ]
+    for copy in copies:
+        copy.start()
+    for copy in copies:
+        copy.wait()
+
+
+def fold_lanes(cap, toks, feat):
+    rest = 2 * cap - toks
+    return -(-feat // (toks // rest * 128)) * 128 if 0 < rest <= toks else 0
 
 
 def fused(cap, pipe_n, expert_n, tensor_n, tokens, expert_ids, gates, w_gate, w_up, w_down, d_out):
@@ -294,31 +366,31 @@
     hidn = w_gate.shape[2]
     rows = expert_n * cap
     xr = (rows + 15) // 16 * 16
-    span = 2 * toks
+    wide = feat + fold_lanes(cap, toks, feat)
     vm = lambda *shape: pltpu.VMEM(shape, BF16)
     vf = lambda *shape: pltpu.VMEM(shape, F32)
     dma = lambda *shape: pltpu.SemaphoreType.DMA(shape)
     inside, outside = pl.BlockSpec(memory_space=pltpu.VMEM), pl.BlockSpec(memory_space=pl.ANY)
-    return pl.pallas_call(
+    results = pl.pallas_call(
         functools.partial(layer_kernel, cap, pipe_n, expert_n, tensor_n),
         out_shape=(
             jax.ShapeDtypeStruct(tokens.shape, BF16),
             jax.ShapeDtypeStruct(tokens.shape, BF16),
-            jax.ShapeDtypeStruct(gates.shape, F32),
+            jax.ShapeDtypeStruct(gates.shape[::-1], F32),
         ),
         in_specs=[inside, inside, inside, outside, outside, outside, inside],
         out_specs=(inside, inside, inside),
         scratch_shapes=[
             vm(8, feat, hidn), vm(8, feat, hidn), vm(8, hidn, feat),
-            vm(expert_n * span, feat), vm(expert_n * span, feat), vm(8, 2 * rows, feat),
+            vm(expert_n * toks, wide), vm(expert_n * toks, wide), vm(8, 2 * rows, feat),
             vf(xr, hidn), vf(xr, hidn), vf(xr, hidn),
             vm(rows, hidn), vm(rows, hidn), vm(rows, hidn),
             vm(6, 2 * rows, feat), vm(4, 2 * rows, feat), vf(2 * rows, feat),
             vm(2 * rows, feat), vm(2 * rows, feat), vf(2 * rows, feat), vf(2 * rows, feat),
             vm(2 * rows, feat), vm(2 * rows, feat),
             vf(8, 128), vf(8, 8, 128), vf(8, 128), vf(expert_n, 8, 128),
-            vm(expert_n * span, feat), vm(expert_n * span, feat),
-            dma(8, 3), dma(expert_n - 1), dma(expert_n - 1), dma(8), dma(8), dma(4), dma(4),
+            vm(expert_n * toks, wide), vm(expert_n * toks, wide),
+            dma(8, 3), dma(expert_n - 1), dma(expert_n - 1), dma(10), dma(10), dma(4), dma(4),
             dma(2), dma(2), dma(4), dma(4), dma(7), dma(7), dma(expert_n - 1), dma(expert_n - 1),
             dma(expert_n - 1), dma(expert_n - 1),
         ],
@@ -329,7 +401,17 @@
             flops=12 * rows * 8 * feat * hidn, bytes_accessed=48 * feat * hidn, transcendentals=rows * hidn
         ),
         name="moe_layer",
-    )(tokens, expert_ids, gates, w_gate, w_up, w_down, d_out)
+    )(tokens, expert_ids.T, gates.T, w_gate, w_up, w_down, d_out)
+    moe_out, grad_tokens, grad_gates = pl.pallas_call(
+        finish_kernel,
+        out_shape=tuple(jax.ShapeDtypeStruct(r.shape, r.dtype) for r in results),
+        in_specs=[outside] * 3,
+        out_specs=(outside,) * 3,
+        scratch_shapes=[dma(3)],
+        compiler_params=pltpu.CompilerParams(vmem_limit_bytes=60 * 1024 * 1024),
+        name="hand_over",
+    )(*results)
+    return moe_out, grad_tokens, grad_gates.T
 
 
 def per_device(tokens, expert_ids, gates, w_gate, w_up, w_down, d_out):
@@ -433,6 +515,9 @@
         cap = min(toks, max(2, max(5 * toks * top // (4 * expert_n), (toks * top + expert_n - 1) // expert_n)))
         rows = expert_n * cap
         fits = pipe_n == 4 and tensor_n == 2 and top == 2 and expert_n == 4
+        feat = args[0].shape[1]
+        piece = fold_lanes(cap, toks, feat)
+        fits = fits and cap < toks and piece > 0 and feat % piece == 0
         if fits and toks % 16 == 0 and rows % 8 == 0 and rows <= 128:
             return fused(cap, pipe_n, expert_n, tensor_n, *args)
         return per_device(*args)

time: 51.7 us -> 46.3 us (0.90)
  local copies, waits for them, and re-layouts: 6.73 us -> 0 us
  Pallas kernels: 43.9 us -> 45.5 us
    unnamed x4 -> x0, local copies, waits for them, and re-layouts: 5.4 us -> none
    pallas_call x0 -> x1, Pallas kernels: none -> 2.65 us  [fused(): pl.pallas_call(finish_kernel, out_shape=tuple((jax.ShapeDtypeStruct(r.sha...]
    pallas_call x1 -> x0, local copies, waits for them, and re-layouts: 1.33 us -> none  [fused(): pl.pallas_call(functools.partial(layer_kernel, cap, pipe_n, expert_n, ten...]
    pallas_call x1, Pallas kernels: 43.9 us -> 42.8 us  [fused(): pl.pallas_call(functools.partial(layer_kernel, cap, pipe_n, expert_n, ten...]
where the time goes in v2:
time: 46.3 us; the launch traced here: 46.1 us
  Pallas kernels  45.5 us (98%)
  between operations  0.64 us (1%)
    pallas_call x1, Pallas kernels, fused(): pl.pallas_call(functools.partial(layer_kernel, cap, pipe_n, expert_n, ten...  42.8 us
    pallas_call x1, Pallas kernels, fused(): pl.pallas_call(finish_kernel, out_shape=tuple((jax.ShapeDtypeStruct(r.sha...  2.65 us

profile of v2, /device:TPU:0, one launch (start us, length us, event | category | flops | bytes accessed | tf_op | source)
XLA Modules:
  0.0 46.1 jit_solution(10867777239836305580)
XLA Ops:
  0.6 42.8 %moe_layer.1 = (bf16[16,768]{1,0:T(8,128)(2,1)}, bf16[16,768]{1,0:T(8,128)(2,1)}, f32[2,16]{1,0:T(2,128)}) custom-call(bf16[16,768]{1,0:T(8,128)(2,1)} %tok_ref.1, s32[2,16]{1,0:T(2,128)} %bitcast.3, f32[2,16]{1,0:T(2,128)} %bitcast.4, bf16[1,6144,1024]{2,1,0:T(8,128)(2,1)} %wg_ref.1, bf16[1,6144,1024]{2,1,0:T(8,128)(2,1)} %wu_ref.1, ...), custom_call_target="tpu_custom_call" | custom-call | flops 3019898880 | bytes 37748736 | tf_op jit(solution)/shard_map/moe_layer/pallas_call | solution.py:374
  43.5 2.7 %hand_over.1 = (bf16[16,768]{1,0:T(8,128)(2,1)}, bf16[16,768]{1,0:T(8,128)(2,1)}, f32[2,16]{1,0:T(2,128)}) custom-call(bf16[16,768]{1,0:T(8,128)(2,1)} %get-tuple-element.9.a, bf16[16,768]{1,0:T(8,128)(2,1)} %get-tuple-element.10.b, f32[2,16]{1,0:T(2,128)} %get-tuple-element.11.c), custom_call_target="tpu_custom_call" | custom-call | tf_op jit(solution)/shard_map/hand_over/pallas_call | solution.py:405
